TPU v7x, 32 devices: a whole 2x2x4 slice. The times are simulated.
32 devices in a mesh: row: 8 (over y, x, core), col: 4 (over z).
Axes of the slice: x: 2, y: 2, z: 4, core: 2. Of those that a mesh axis runs over, the one named last changes fastest.
Arguments:
- embeddings: float32 [1024, 768], P(('row', 'col')), may hold values from -0.21650635 to 0.21650635
- sharpness: float32 [1024], P(('row', 'col')), may hold values from 0.5 to 4
- soft_labels: float32 [1024, 256], P(('row', 'col')), may hold values from 0 to 1
- seed_mask: int32 [1024], P(('row', 'col')), may hold values 0 or 1
- tile_mask: int32 [32, 32], P('row'), may hold values from 0 to 1, as said below
Outputs:
- spread_labels: float32 [1024, 256], P(('row', 'col'))
Inputs may be any that keep to these rules, and one draw needn't show every extreme that they name: Every diagonal entry tile_mask[p, p] is 1.
All inputs are finite; a program needn't handle non-finite values. No bound on the sum of `seed_mask` on one device may be relied on, other than what follows from the above.
Results may differ from a plain program's by a relative error of at most 0.0003.
Values sent between devices are 32-bit elements; how exact they have to be, the bound alone decides.
A program may use at most 64 MiB of HBM per device.

v0:
```python
import jax
import jax.numpy as jnp
from jax import lax
from jax.sharding import PartitionSpec as P

ITERS = 3


def kernel_tile(row_emb, row_squares, row_width, col_emb, col_width, col_mask):
    cross = jnp.dot(
        row_emb, col_emb.T, precision=lax.Precision.HIGHEST, preferred_element_type=jnp.float32
    )
    col_squares = jnp.sum(col_emb * col_emb, axis=1)
    distance = row_squares[:, None] + col_squares[None, :] - 2.0 * cross
    return jnp.exp(-(distance * row_width[:, None] * col_width[None, :])) * col_mask


def local(embeddings, sharpness, soft_labels, seed_mask, tile_mask):
    n_row = lax.axis_size("row")
    n_col = lax.axis_size("col")
    col_index = lax.axis_index("col")
    piece = embeddings.shape[0]
    seeded = seed_mask.astype(jnp.float32)[:, None] * soft_labels
    row_emb, row_width = (
        lax.all_gather(embeddings, "col", axis=0, tiled=True),
        lax.all_gather(sharpness, "col", axis=0, tiled=True),
    )
    row_squares = jnp.sum(row_emb * row_emb, axis=1)
    block_rows = row_emb.shape[0]
    col_rows = piece * n_row
    grouped = tile_mask.reshape(n_col, n_row, n_col)
    chosen = lax.dynamic_index_in_dim(grouped, col_index, axis=2, keepdims=False)
    col_mask = jnp.broadcast_to(chosen[:, None, :, None], (n_col, piece, n_row, piece))
    col_mask = col_mask.reshape(block_rows, col_rows).astype(jnp.float32)
    col_emb, col_width = (
        lax.all_gather(embeddings, "row", axis=0, tiled=True),
        lax.all_gather(sharpness, "row", axis=0, tiled=True),
    )
    labels = seeded
    for iteration in range(ITERS):
        col_labels = lax.all_gather(labels, "row", axis=0, tiled=True)
        weights = kernel_tile(row_emb, row_squares, row_width, col_emb, col_width, col_mask)
        partial_value = jnp.dot(
            weights, col_labels, precision=lax.Precision.HIGHEST, preferred_element_type=jnp.float32
        )
        degree = jnp.sum(weights, axis=1)
        total_part, total_degree = lax.psum((partial_value, degree), "col")
        own_part = lax.dynamic_slice_in_dim(total_part, col_index * piece, piece, 0)
        own_degree = lax.dynamic_slice_in_dim(total_degree, col_index * piece, piece, 0)
        labels = 0.9 * own_part / own_degree[:, None] + 0.1 * seeded
    return labels


def solution(mesh):
    return jax.shard_map(
        local,
        mesh=mesh,
        in_specs=(
            P(("row", "col"), None),
            P(("row", "col")),
            P(("row", "col"), None),
            P(("row", "col")),
            P("row", None),
        ),
        out_specs=P(("row", "col"), None),
        check_vma=False,
    )
```

profile of v0, /device:TPU:0, one launch (start us, length us, event | category | flops | bytes accessed | tf_op | source)
XLA Modules:
  0.0 204.2 jit_solution(2896193417562795087)
XLA Ops:
  6.5 0.0 all-reduce.6.cloned.1.call-start
  6.5 0.0 copy-start.1
  6.5 12.3 %all_gather.22 = f32[256,768]{1,0:T(8,128)S(1)} all-gather(f32[32,768]{1,0:T(8,128)} %param.5), channel_id=1, replica_groups=mesh['row'=8,'col'=4] {'row'}, dimensions={0}, use_global_device_ids=true | all-gather | bytes 884736 | tf_op jit(solution)/shard_map/all_gather | solution.py:36
  18.9 0.0 copy-done.1
  18.9 14.9 %all_gather.21 = f32[128,768]{1,0:T(8,128)S(1)} all-gather(f32[32,768]{1,0:T(8,128)S(1)} %copy-done.1), channel_id=1, replica_groups=mesh['row'=8,'col'=4] {'col'}, dimensions={0}, use_global_device_ids=true | all-gather | bytes 491520 | tf_op jit(solution)/shard_map/all_gather | solution.py:25
  33.8 0.0 copy-start.2
  33.8 0.7 copy-done.2
  34.5 0.1 reshape.14
  34.5 0.2 convert_reduce_fusion
  34.7 0.1 broadcast_in_dim.2
  34.8 0.2 convert_element_type.15
  35.0 0.0 copy-start.6
  35.0 0.6 copy-done.6
  35.7 0.6 dynamic-slice.1
  36.9 0.0 copy-start.3
  36.9 0.6 copy-done.3
  37.6 0.2 dynamic-update-slice.1
  37.7 0.0 copy-start.5
  37.7 11.9 %all-reduce.1 = f32[256]{0:T(256)S(1)} all-reduce(f32[256]{0:T(256)S(1)} %dynamic-update-slice.1), channel_id=1, replica_groups=mesh['row'=8,'col'=4] {'row'}, use_global_device_ids=true, to_apply=%add.1 | all-reduce | flops 256 | bytes 2048
  49.7 0.0 copy-done.5
  49.7 0.6 dynamic-slice
  50.9 0.2 dynamic-update-slice
  51.1 12.4 %all-reduce = f32[128]{0:T(128)S(1)} all-reduce(f32[128]{0:T(128)S(1)} %dynamic-update-slice), channel_id=1, replica_groups=mesh['row'=8,'col'=4] {'col'}, use_global_device_ids=true, to_apply=%add | all-reduce | flops 128 | bytes 1024
  63.6 0.1 multiply_reduce_fusion
  63.7 0.0 copy-start.4
  63.7 0.0 copy-start
  63.7 0.1 multiply_reduce_fusion.1
  63.8 0.5 copy-done.4
  64.4 0.1 copy-done
  64.5 0.1 broadcast_multiply_fusion
  64.6 8.9 %all_gather.25 = f32[256,256]{1,0:T(8,128)S(1)} all-gather(f32[32,256]{1,0:T(8,128)S(1)} %broadcast_multiply_fusion), channel_id=1, replica_groups=mesh['row'=8,'col'=4] {'row'}, dimensions={0}, use_global_device_ids=true | all-gather | bytes 294912 | tf_op jit(solution)/shard_map/all_gather | solution.py:41
  73.5 1.0 fusion.6
  74.5 0.9 fusion.7
  75.5 0.0 all-reduce.6.cloned.1.call-update
  75.5 0.0 all-reduce.8.cloned.1.call-start
  75.5 8.4 %psum.29 = f32[128]{0:T(128)S(1)} all-reduce(f32[128]{0:T(128)S(1)} %get-tuple-element.5), channel_id=1, replica_groups=mesh['row'=8,'col'=4] {'col'}, use_global_device_ids=true, to_apply=%region_4.5 | all-reduce | flops 128 | bytes 1024 | tf_op jit(solution)/shard_map/psum | solution.py:47
  83.9 0.1 dynamic_slice.20
  84.0 23.4 %all-reduce.6.cloned.1.call-done = f32[128,256]{1,0:T(8,128)} async-done(((f32[128,256]{1,0:T(8,128)}), f32[128,256]{1,0:T(8,128)}) %all-reduce.6.cloned.1.call-update) | async-done | bytes 131088 | tf_op jit(solution)/shard_map/psum | solution.py:47
  107.4 0.8 divide_add_fusion.2
  108.2 9.2 %all_gather.26 = f32[256,256]{1,0:T(8,128)S(1)} all-gather(f32[32,256]{1,0:T(8,128)S(1)} %divide_add_fusion.2), channel_id=1, replica_groups=mesh['row'=8,'col'=4] {'row'}, dimensions={0}, use_global_device_ids=true | all-gather | bytes 294912 | tf_op jit(solution)/shard_map/all_gather | solution.py:41
  117.4 0.9 fusion.8
  118.4 0.0 all-reduce.8.cloned.1.call-update
  118.4 0.0 all-reduce.10.cloned.1.call-start
  118.5 33.4 %all-reduce.8.cloned.1.call-done = f32[128,256]{1,0:T(8,128)} async-done(((f32[128,256]{1,0:T(8,128)}), f32[128,256]{1,0:T(8,128)}) %all-reduce.8.cloned.1.call-update) | async-done | bytes 131088 | tf_op jit(solution)/shard_map/psum | solution.py:47
  151.8 0.8 divide_add_fusion.1
  152.7 9.2 %all_gather.27 = f32[256,256]{1,0:T(8,128)S(1)} all-gather(f32[32,256]{1,0:T(8,128)S(1)} %divide_add_fusion.1), channel_id=1, replica_groups=mesh['row'=8,'col'=4] {'row'}, dimensions={0}, use_global_device_ids=true | all-gather | bytes 294912 | tf_op jit(solution)/shard_map/all_gather | solution.py:41
  161.9 0.9 fusion.9
  162.8 0.0 all-reduce.10.cloned.1.call-update
  162.8 33.4 %all-reduce.10.cloned.1.call-done = f32[128,256]{1,0:T(8,128)} async-done(((f32[128,256]{1,0:T(8,128)}), f32[128,256]{1,0:T(8,128)}) %all-reduce.10.cloned.1.call-update) | async-done | bytes 131088 | tf_op jit(solution)/shard_map/psum | solution.py:47
  196.3 1.5 divide_add_fusion
  (3 shorter events, 0.0 us)
Async XLA Ops:
  6.5 100.8 %all-reduce.6.cloned.1.call-start = ((), (), s32[]{:S(2)}) async-start(), calls=%async_computation | async-start | bytes 262144 | tf_op jit(solution)/shard_map/psum | solution.py:47
  6.5 12.3 %copy-start.1 = (f32[32,768]{1,0:T(8,128)S(1)}, f32[32,768]{1,0:T(8,128)}, u32[]{:S(2)}) copy-start(f32[32,768]{1,0:T(8,128)} %param.5) | copy-start | bytes 294916
  33.8 0.7 copy-start.2
  35.0 0.7 copy-start.6
  36.9 0.7 copy-start.3
  37.7 11.9 %copy-start.5 = (u32[32]{0:T(128)S(1)}, u32[32]{0:T(128)}, u32[]{:S(2)}) copy-start(u32[32]{0:T(128)} %constant.26) | copy-start | bytes 388
  63.7 0.7 copy-start.4
  63.7 0.8 copy-start
  75.5 76.3 %all-reduce.8.cloned.1.call-start = ((), (), s32[]{:S(2)}) async-start(), calls=%async_computation.1 | async-start | bytes 262144 | tf_op jit(solution)/shard_map/psum | solution.py:47
  118.4 77.9 %all-reduce.10.cloned.1.call-start = ((), (), s32[]{:S(2)}) async-start(), calls=%async_computation.2 | async-start | bytes 262144 | tf_op jit(solution)/shard_map/psum | solution.py:47
Sparse Core Ops, SparseCore 0:
  75.6 31.7 all-reduce.5
  118.5 33.2 all-reduce.7
  163.0 33.2 all-reduce.9
where the time goes:
time: 205 us; the launch traced here: 204 us
  waiting for transfers between devices  90.2 us (44%)
  blocking collectives  87.4 us (43%)
  between operations  14.5 us (7%)
  local copies, waits for them, and re-layouts  4.66 us (2%)
  matrix products  3.83 us (2%)
  other arithmetic  3.59 us (2%)
    psum x3, waiting for transfers between devices, local(): total_part, total_degree = lax.psum((partial_value, degree), 'col')  90.2 us
    all_gather x3, blocking collectives, local(): col_labels = lax.all_gather(labels, 'row', axis=0, tiled=True)  27.4 us
    unnamed x2, blocking collectives  24.3 us
    all_gather x1, blocking collectives, local(): lax.all_gather(embeddings, 'col', axis=0, tiled=True)  14.9 us
    all_gather x1, blocking collectives, local(): lax.all_gather(embeddings, 'row', axis=0, tiled=True)  12.3 us
    psum x1, blocking collectives, local(): total_part, total_degree = lax.psum((partial_value, degree), 'col')  8.38 us
    unnamed x20, local copies, waits for them, and re-layouts  4.21 us
  transfers between devices with their start and end apart: 3, of which 3 were waited for; matrix products, arithmetic and copies ran while one was open for 0% of the time, Pallas kernels for 0%

commit v1 on v0

v1 whole, which is shorter than its diff:
```python
import functools

import jax
import jax.numpy as jnp
from jax import lax
from jax.experimental import pallas as pl
from jax.experimental.pallas import tpu as pltpu
from jax.sharding import PartitionSpec as P

ITERS = 3
MESH = pl.DeviceIdType.MESH
EXACT = lax.Precision.HIGHEST
AUX = 8


def dot(a, b, a_dim=1, b_dim=0):
    return lax.dot_general(
        a, b, (((a_dim,), (b_dim,)), ((), ())), precision=EXACT, preferred_element_type=jnp.float32
    )


def iota(shape, dim):
    return lax.broadcasted_iota(jnp.int32, shape, dim)


def to_column(line):
    n = line.shape[1]
    eye = iota((n, n), 0) == iota((n, n), 1)
    return jnp.sum(jnp.where(eye, jnp.broadcast_to(line, (n, n)), 0.0), axis=1, keepdims=True)


def kernel(
    chips, cols, emb_ref, sharp_ref, soft_ref, seed_ref, tile_ref, out_ref,
    row_emb, col_emb, row_aux, mask_buf, first, later, part, summed, last_part, last, weights, send,
    row_sem, col_sem, aux_sem, mask_sem, first_sem, later_sem, sum_sem, last_sem, send_sem,
):
    piece, width = emb_ref.shape
    half = soft_ref.shape[1] // 2
    rows = 2 * chips
    r, z = lax.axis_index("row"), lax.axis_index("col")
    chip, core = r // 2, lax.rem(r, 2)
    twin = r + 1 - 2 * core
    mine = 2 * z + core

    others_z = [lax.rem(z + d, cols) for d in range(1, cols)]
    others_chip = [lax.rem(chip + d, chips) for d in range(1, chips)]
    peers = [(twin, z)]
    peers += [(2 * chip + k, other) for other in others_z for k in range(2)]
    peers += [(2 * other + k, z) for other in others_chip for k in range(2)]

    barrier = pltpu.get_barrier_semaphore()
    for peer in peers:
        pl.semaphore_signal(barrier, inc=1, device_id=peer, device_id_type=MESH)

    sharp = sharp_ref[...]
    seeded = to_column(seed_ref[...].astype(jnp.float32)) * soft_ref[...]
    aux = jnp.concatenate([sharp, jnp.zeros((1, 128 - piece), jnp.float32)], axis=1)
    aux = jnp.broadcast_to(aux, (AUX, 128))
    row_aux[mine] = aux
    for k in range(2):
        send[k, :piece] = seeded[:, k * half : (k + 1) * half]
        send[k, piece:, :] = jnp.broadcast_to(aux[:, :1], (AUX, half)) if half < 128 else jnp.concatenate(
            [aux] + [jnp.zeros((AUX, half - 128), jnp.float32)] * (half > 128), axis=1
        )
    mask_buf[core] = jnp.zeros(mask_buf.shape[1:], jnp.float32)
    mask_buf[core, : tile_ref.shape[0], : tile_ref.shape[1]] = tile_ref[...].astype(jnp.float32)
    pl.semaphore_wait(barrier, len(peers))

    sent = []

    def push(src, dst, recv, peer):
        copy = pltpu.make_async_remote_copy(
            src_ref=src, dst_ref=dst, send_sem=send_sem.at[len(sent)], recv_sem=recv,
            device_id=peer, device_id_type=MESH,
        )
        copy.start()
        sent.append(copy)

    def arrived(dst, recv):
        pltpu.make_async_remote_copy(
            src_ref=dst, dst_ref=dst, send_sem=send_sem.at[0], recv_sem=recv,
            device_id=(twin, z), device_id_type=MESH,
        ).wait_recv()

    for other in others_z:
        push(emb_ref, row_emb.at[mine], row_sem.at[mine], (r, other))
    for other in others_chip:
        push(emb_ref, col_emb.at[r], col_sem.at[r], (2 * other + core, z))
    push(emb_ref, row_emb.at[mine], row_sem.at[mine], (twin, z))
    push(emb_ref, col_emb.at[r], col_sem.at[r], (twin, z))
    push(row_aux.at[mine], row_aux.at[mine], aux_sem.at[mine], (twin, z))
    for other in others_z:
        for k in range(2):
            push(row_aux.at[mine], row_aux.at[mine], aux_sem.at[mine], (2 * chip + k, other))
    push(send.at[1 - core], first.at[r], first_sem.at[r], (twin, z))
    for other in others_chip:
        for k in range(2):
            push(send.at[k], first.at[r], first_sem.at[r], (2 * other + k, z))
    push(mask_buf.at[core], mask_buf.at[core], mask_sem, (twin, z))

    row_emb[mine] = emb_ref[...]
    col_emb[r] = emb_ref[...]
    first[r] = send[core]

    for other in others_chip:
        slot = 2 * other + core
        arrived(col_emb.at[slot], col_sem.at[slot])
        push(col_emb.at[slot], col_emb.at[slot], col_sem.at[slot], (twin, z))
    for other in others_z:
        slot = 2 * other + core
        arrived(row_emb.at[slot], row_sem.at[slot])
        push(row_emb.at[slot], row_emb.at[slot], row_sem.at[slot], (twin, z))

    arrived(mask_buf.at[1 - core], mask_sem)
    for other in [z] + others_z:
        for k in range(2):
            slot = 2 * other + k
            if other is z:
                if k == 0:
                    arrived(row_aux.at[2 * z + 1 - core], aux_sem.at[2 * z + 1 - core])
            else:
                arrived(row_aux.at[slot], aux_sem.at[slot])
    arrived(first.at[twin], first_sem.at[twin])
    for other in others_chip:
        for k in range(2):
            arrived(first.at[2 * other + k], first_sem.at[2 * other + k])

    n_rows, n_cols = 2 * cols * piece, rows * piece
    mask_rows, tiles = 2 * mask_buf.shape[1], mask_buf.shape[2]
    wanted = (iota((tiles, n_cols), 1) // piece) * cols + z
    pick_cols = (iota((tiles, n_cols), 0) == wanted).astype(jnp.float32)
    col_mask = dot(mask_buf[...].reshape(mask_rows, tiles), pick_cols)
    line = first[:, piece:, :128].reshape(rows * AUX, 128)[:, :piece]
    at = iota((piece, n_cols), 1)
    spread = dot(line, (iota((piece, n_cols), 0) == lax.rem(at, piece)).astype(jnp.float32))
    at = iota((rows * AUX, n_cols), 1)
    keep = iota((rows * AUX, n_cols), 0) == (at // piece) * AUX
    col_sharp = jnp.sum(jnp.where(keep, spread, 0.0), axis=0, keepdims=True)

    arrived(col_emb.at[twin], col_sem.at[twin])
    for other in others_chip:
        slot = 2 * other + 1 - core
        arrived(col_emb.at[slot], col_sem.at[slot])
    theirs = col_emb[...].reshape(n_cols, width)
    col_squares = dot(jnp.ones((8, width), jnp.float32), theirs * theirs, 1, 1)[:1]
    arrived(row_emb.at[2 * z + 1 - core], row_sem.at[2 * z + 1 - core])
    for other in others_z:
        slot = 2 * other + 1 - core
        arrived(row_emb.at[slot], row_sem.at[slot])

    group = min(2 * cols, max(1, 256 // piece))

    def block(b):
        at = b * group
        ours = row_emb[pl.ds(at, group)].reshape(group * piece, width)
        cross = dot(ours, theirs, 1, 1)
        squares = jnp.sum(ours * ours, axis=1, keepdims=True)
        sharp_at = row_aux[pl.ds(at, group)]
        row_sharp = jnp.concatenate([to_column(sharp_at[g, :1, :piece]) for g in range(group)], axis=0)
        tile = iota((group * piece, mask_rows), 0) // piece + at
        wanted = lax.rem(tile, 2) * (mask_rows // 2) + tile // 2
        pick = (iota((group * piece, mask_rows), 1) == wanted).astype(jnp.float32)
        distance = squares + col_squares - 2.0 * cross
        value = jnp.exp(-(distance * row_sharp * col_sharp)) * dot(pick, col_mask)
        weights[pl.ds(b * group * piece, group * piece)] = value

    if group == 2 * cols:
        block(0)
    else:
        pl.loop(0, 2 * cols // group)(block)

    pair = 2 * piece
    kept = jnp.concatenate([first[2 * chip, :piece], first[2 * chip + 1, :piece]], axis=0)
    degree = None
    for step in range(ITERS):
        if step == 0:
            labels = first[:, :piece].reshape(n_cols, half)
        else:
            labels = later[step - 1].reshape(n_cols, half)
        if step < ITERS - 1:
            for c in range(cols):
                ours = weights[c * pair : (c + 1) * pair]
                part[step, c, :pair] = dot(ours, labels)
                if step == 0:
                    sums = dot(jnp.ones((AUX, n_cols), jnp.float32), ours, 1, 1)
                    part[step, c, pair:, :pair] = sums
            depth = pair + AUX if step == 0 else pair
            for other in others_z:
                push(
                    part.at[step, other, pl.ds(0, depth)], summed.at[step, z, pl.ds(0, depth)],
                    sum_sem.at[step, z], (r, other),
                )
            total = part[step, z, :depth]
            for other in others_z:
                arrived(summed.at[step, other, pl.ds(0, depth)], sum_sem.at[step, other])
                total = total + summed[step, other, :depth]
            if step == 0:
                degree = to_column(total[pair : pair + 1, :pair])
            new = 0.9 * total[:pair] / degree + 0.1 * kept
            later[step, chip] = new
            for other in others_chip:
                push(
                    later.at[step, chip], later.at[step, chip], later_sem.at[step, chip],
                    (2 * other + core, z),
                )
            for other in others_chip:
                arrived(later.at[step, other], later_sem.at[step, other])
        else:
            for c in range(cols):
                value = dot(weights[c * pair : (c + 1) * pair], labels)
                last_part[c] = value.reshape(2, piece, half)
            push(last_part.at[z, 1 - core], last.at[z, core], last_sem.at[z, core], (twin, z))
            for other in others_z:
                for k in range(2):
                    push(last_part.at[other, k], last.at[z, core], last_sem.at[z, core], (2 * chip + k, other))
            last[z, core] = last_part[z, core]
            arrived(last.at[z, 1 - core], last_sem.at[z, 1 - core])
            for other in others_z:
                for k in range(2):
                    arrived(last.at[other, k], last_sem.at[other, k])
            total = jnp.sum(last[...], axis=0)
            own = jnp.where(core == 0, degree[:piece], degree[piece:])
            for k in range(2):
                out_ref[:, k * half : (k + 1) * half] = (
                    0.9 * total[k] / own + 0.1 * send[k, :piece]
                )
    for copy in sent:
        copy.wait_send()


def round_up(n, m):
    return (n + m - 1) // m * m


def local(chips, cols, embeddings, sharpness, soft_labels, seed_mask, tile_mask):
    piece, width = embeddings.shape
    half = soft_labels.shape[1] // 2
    rows = 2 * chips
    tile_rows, tiles = round_up(tile_mask.shape[0], 8), round_up(tile_mask.shape[1], 128)
    pair = 2 * piece
    sends = (
        2 * (cols - 1) + 2 * (chips - 1) + 2 + 1 + 2 * (cols - 1) + 1 + 2 * (chips - 1) + 1
        + (ITERS - 1) * (cols + chips - 2) + 2 * cols - 1
    )
    f32, dma = jnp.float32, pltpu.SemaphoreType.DMA
    vmem = pl.BlockSpec(memory_space=pltpu.VMEM)
    return pl.pallas_call(
        functools.partial(kernel, chips, cols),
        out_shape=jax.ShapeDtypeStruct(soft_labels.shape, f32),
        in_specs=[vmem] * 5,
        out_specs=vmem,
        scratch_shapes=[
            pltpu.VMEM((2 * cols, piece, width), f32),
            pltpu.VMEM((rows, piece, width), f32),
            pltpu.VMEM((2 * cols, AUX, 128), f32),
            pltpu.VMEM((2, tile_rows, tiles), f32),
            pltpu.VMEM((rows, piece + AUX, half), f32),
            pltpu.VMEM((ITERS - 1, chips, pair, half), f32),
            pltpu.VMEM((ITERS - 1, cols, pair + AUX, half), f32),
            pltpu.VMEM((ITERS - 1, cols, pair + AUX, half), f32),
            pltpu.VMEM((cols, 2, piece, half), f32),
            pltpu.VMEM((cols, 2, piece, half), f32),
            pltpu.VMEM((2 * cols * piece, rows * piece), f32),
            pltpu.VMEM((2, piece + AUX, half), f32),
            dma((2 * cols,)),
            dma((rows,)),
            dma((2 * cols,)),
            dma(()),
            dma((rows,)),
            dma((ITERS - 1, chips)),
            dma((ITERS - 1, cols)),
            dma((cols, 2)),
            dma((sends,)),
        ],
        compiler_params=pltpu.CompilerParams(
            collective_id=0, has_side_effects=True, vmem_limit_bytes=48 * 1024 * 1024
        ),
    )(embeddings, sharpness.reshape(1, piece), soft_labels, seed_mask.reshape(1, piece), tile_mask)


def solution(mesh):
    return jax.shard_map(
        functools.partial(local, mesh.shape["row"] // 2, mesh.shape["col"]),
        mesh=mesh,
        in_specs=(
            P(("row", "col"), None),
            P(("row", "col")),
            P(("row", "col"), None),
            P(("row", "col")),
            P("row", None),
        ),
        out_specs=P(("row", "col"), None),
        check_vma=False,
    )
```

time: 205 us -> 45.1 us (0.22)
  waiting for transfers between devices: 90.2 us -> 0 us
  blocking collectives: 87.4 us -> 0 us
  Pallas kernels: 0 us -> 41.9 us
  between operations: 14.5 us -> 0.01 us
  matrix products: 3.83 us -> 0 us
  other arithmetic: 3.59 us -> 0 us
    psum x3 -> x0, waiting for transfers between devices: 90.2 us -> none  [local(): total_part, total_degree = lax.psum((partial_value, degree), 'col')]
    all_gather x5 -> x0, blocking collectives: 54.6 us -> none  [the longest x3 27.4 us: local(): col_labels = lax.all_gather(labels, 'row', axis=0, tiled=True)]
    pallas_call x0 -> x1, Pallas kernels: none -> 41.9 us  [local(): pl.pallas_call(functools.partial(kernel, chips, cols), out_shape=jax.Shap...]
    unnamed x2 -> x0, blocking collectives: 24.3 us -> none
    psum x1 -> x0, blocking collectives: 8.38 us -> none  [local(): total_part, total_degree = lax.psum((partial_value, degree), 'col')]
    dot_general x4 -> x0, matrix products: 3.83 us -> none  [the longest x3 2.82 us: local(): jnp.dot(weights, col_labels, precision=lax.Precision.HIGHEST, preferred_e...]
    add x3 -> x0, other arithmetic: 3.12 us -> none  [local(): labels = 0.9 * own_part / own_degree[:, None] + 0.1 * seeded]
    unnamed x20 -> x11, local copies, waits for them, and re-layouts: 4.21 us -> 2.95 us
  transfers between devices with their start and end apart: 3 -> 0, of which waited for: 3 -> 0; matrix products, arithmetic and copies ran while one was open for 0% -> 0% of each run, Pallas kernels for 0% -> 0%
where the time goes in v1:
time: 45.1 us; the launch traced here: 44.9 us
  Pallas kernels  41.9 us (93%)
  local copies, waits for them, and re-layouts  2.95 us (7%)
    pallas_call x1, Pallas kernels, local(): pl.pallas_call(functools.partial(kernel, chips, cols), out_shape=jax.Shap...  41.9 us
    unnamed x11, local copies, waits for them, and re-layouts  2.95 us

profile of v1, /device:TPU:0, one launch (start us, length us, event | category | flops | bytes accessed | tf_op | source)
XLA Modules:
  0.0 44.9 jit_solution(13024734641398505269)
XLA Ops:
  0.0 0.0 copy-start.2
  0.0 0.0 copy-start.3
  0.0 0.0 copy-start.4
  0.0 0.7 %copy-done.2 = s32[4,32]{1,0:T(4,128)S(1)} copy-done((s32[4,32]{1,0:T(4,128)S(1)}, s32[4,32]{1,0:T(4,128)}, u32[]{:S(2)}) %copy-start.2) | copy-done | bytes 536
  0.7 0.0 copy-done.3
  0.7 0.0 copy-done.4
  0.7 0.0 copy-start
  0.7 0.9 %copy-done = f32[32,768]{1,0:T(8,128)S(1)} copy-done((f32[32,768]{1,0:T(8,128)S(1)}, f32[32,768]{1,0:T(8,128)}, u32[]{:S(2)}) %copy-start) | copy-done | bytes 98328
  1.6 0.0 copy-start.1
  1.6 0.8 %copy-done.1 = f32[32,256]{1,0:T(8,128)S(1)} copy-done((f32[32,256]{1,0:T(8,128)S(1)}, f32[32,256]{1,0:T(8,128)}, u32[]{:S(2)}) %copy-start.1) | copy-done | bytes 32792
  2.3 41.9 %shard_map.55 = f32[32,256]{1,0:T(8,128)S(1)} custom-call(f32[32,768]{1,0:T(8,128)S(1)} %copy-done, f32[1,32]{1,0:T(1,128)S(1)} %bitcast.2, f32[32,256]{1,0:T(8,128)S(1)} %copy-done.1, s32[1,32]{1,0:T(1,128)S(1)} %bitcast.3, s32[4,32]{1,0:T(4,128)S(1)} %copy-done.2), custom_call_target="tpu_custom_call" | custom-call | tf_op jit(solution)/shard_map/pallas_call | solution.py:247
  44.2 0.6 %copy.7 = f32[32,256]{1,0:T(8,128)} copy(f32[32,256]{1,0:T(8,128)S(1)} %shard_map.55) | data formatting | bytes 65536
Async XLA Ops:
  0.0 0.7 %copy-start.2 = (s32[4,32]{1,0:T(4,128)S(1)}, s32[4,32]{1,0:T(4,128)}, u32[]{:S(2)}) copy-start(s32[4,32]{1,0:T(4,128)} %tile_ref.1) | copy-start | bytes 1540
  0.0 0.7 %copy-start.3 = (f32[32]{0:T(128)S(1)}, f32[32]{0:T(128)}, u32[]{:S(2)}) copy-start(f32[32]{0:T(128)} %param.6) | copy-start | bytes 388
  0.0 0.7 %copy-start.4 = (s32[32]{0:T(128)S(1)}, s32[32]{0:T(128)}, u32[]{:S(2)}) copy-start(s32[32]{0:T(128)} %param.8) | copy-start | bytes 388
  0.7 0.9 %copy-start = (f32[32,768]{1,0:T(8,128)S(1)}, f32[32,768]{1,0:T(8,128)}, u32[]{:S(2)}) copy-start(f32[32,768]{1,0:T(8,128)} %emb_ref.1) | copy-start | bytes 294916
  1.6 0.8 %copy-start.1 = (f32[32,256]{1,0:T(8,128)S(1)}, f32[32,256]{1,0:T(8,128)}, u32[]{:S(2)}) copy-start(f32[32,256]{1,0:T(8,128)} %soft_ref.1) | copy-start | bytes 98308

commit v2 on v1

v2 whole, which is shorter than its diff:
```python
import functools

import jax
import jax.numpy as jnp
from jax import lax
from jax.experimental import pallas as pl
from jax.experimental.pallas import tpu as pltpu
from jax.sharding import PartitionSpec as P

ITERS = 3
MESH = pl.DeviceIdType.MESH
EXACT = lax.Precision.HIGHEST
AUX = 8


def dot(a, b, a_dim=1, b_dim=0):
    return lax.dot_general(
        a, b, (((a_dim,), (b_dim,)), ((), ())), precision=EXACT, preferred_element_type=jnp.float32
    )


def iota(shape, dim):
    return lax.broadcasted_iota(jnp.int32, shape, dim)


def to_column(line):
    n = line.shape[1]
    eye = iota((n, n), 0) == iota((n, n), 1)
    return jnp.sum(jnp.where(eye, jnp.broadcast_to(line, (n, n)), 0.0), axis=1, keepdims=True)


def to_line(column):
    n = column.shape[0]
    eye = iota((n, n), 0) == iota((n, n), 1)
    return jnp.sum(jnp.where(eye, jnp.broadcast_to(column, (n, n)), 0.0), axis=0, keepdims=True)


def split(value):
    high = value.astype(jnp.bfloat16)
    return high, (value - high.astype(jnp.float32)).astype(jnp.bfloat16)


def quick(a, b, b_dim=0):
    return lax.dot_general(a, b, (((1,), (b_dim,)), ((), ())), preferred_element_type=jnp.float32)


def by_distance(n):
    return sorted(range(1, n), key=lambda d: (min(d, n - d), d))


def kernel(
    chips, cols, emb_ref, sharp_ref, soft_ref, seed_ref, tile_ref, out_ref,
    row_emb, col_emb, row_aux, mask_buf, first, later, part, summed, last_part, last,
    w_high, w_low, c_high, c_low, send, soft, sharp_in, seed_in, tile_in,
    row_sem, col_sem, aux_sem, mask_sem, first_sem, later_sem, sum_sem, last_sem, send_sem, load_sem,
):
    piece, width = emb_ref.shape
    half = soft_ref.shape[1] // 2
    rows = 2 * chips
    pair = 2 * piece
    r, z = lax.axis_index("row"), lax.axis_index("col")
    chip, core = r // 2, lax.rem(r, 2)
    twin = r + 1 - 2 * core
    mine = 2 * z + core

    others_z = [lax.rem(z + d, cols) for d in by_distance(cols)]
    others_chip = [lax.rem(chip + d, chips) for d in by_distance(chips)]
    peers = [(twin, z)]
    peers += [(2 * chip + k, other) for other in others_z for k in range(2)]
    peers += [(2 * other + k, z) for other in others_chip for k in range(2)]

    loads = []
    for src, dst in (
        (emb_ref, row_emb.at[mine]), (soft_ref, soft), (sharp_ref, sharp_in), (seed_ref, seed_in),
        (tile_ref, tile_in), (emb_ref, col_emb.at[r]),
    ):
        loads.append(pltpu.make_async_copy(src, dst, load_sem.at[len(loads)]))
        loads[-1].start()
    barrier = pltpu.get_barrier_semaphore()
    for peer in peers:
        pl.semaphore_signal(barrier, inc=1, device_id=peer, device_id_type=MESH)
    mask_buf[core] = jnp.zeros(mask_buf.shape[1:], jnp.float32)
    for load in loads:
        load.wait()

    sharp = sharp_in[...]
    aux = jnp.concatenate([sharp, jnp.zeros((1, 128 - piece), jnp.float32)], axis=1)
    aux = jnp.broadcast_to(aux, (AUX, 128))
    row_aux[mine] = aux
    mask_buf[core, : tile_ref.shape[0], : tile_ref.shape[1]] = tile_in[...].astype(jnp.float32)
    seeded = to_column(seed_in[...].astype(jnp.float32)) * soft[...]
    for k in range(2):
        send[k, :piece] = seeded[:, k * half : (k + 1) * half]
        send[k, piece:, :128] = aux
    first[r] = send[core]
    pl.semaphore_wait(barrier, len(peers))

    sent = []

    def push(src, dst, recv, peer):
        copy = pltpu.make_async_remote_copy(
            src_ref=src, dst_ref=dst, send_sem=send_sem.at[len(sent)], recv_sem=recv,
            device_id=peer, device_id_type=MESH,
        )
        copy.start()
        sent.append(copy)

    def arrived(dst, recv):
        pltpu.make_async_remote_copy(
            src_ref=dst, dst_ref=dst, send_sem=send_sem.at[0], recv_sem=recv,
            device_id=(twin, z), device_id_type=MESH,
        ).wait_recv()

    for other in others_z:
        push(row_emb.at[mine], row_emb.at[mine], row_sem.at[mine], (r, other))
    for other in others_chip:
        push(col_emb.at[r], col_emb.at[r], col_sem.at[r], (2 * other + core, z))
    push(col_emb.at[r], col_emb.at[r], col_sem.at[r], (twin, z))
    push(row_emb.at[mine], row_emb.at[mine], row_sem.at[mine], (twin, z))
    for other in others_chip:
        for k in range(2):
            push(send.at[k], first.at[r], first_sem.at[r], (2 * other + k, z))
    push(send.at[1 - core], first.at[r], first_sem.at[r], (twin, z))
    push(mask_buf.at[core], mask_buf.at[core], mask_sem, (twin, z))
    push(row_aux.at[mine], row_aux.at[mine], aux_sem.at[mine], (twin, z))
    for other in others_z:
        for k in range(2):
            push(row_aux.at[mine], row_aux.at[mine], aux_sem.at[mine], (2 * chip + k, other))

    for other in others_chip:
        slot = 2 * other + core
        arrived(col_emb.at[slot], col_sem.at[slot])
        push(col_emb.at[slot], col_emb.at[slot], col_sem.at[slot], (twin, z))

    def hand_on(other):
        slot = 2 * other + core
        arrived(row_emb.at[slot], row_sem.at[slot])
        push(row_emb.at[slot], row_emb.at[slot], row_sem.at[slot], (twin, z))

    n_cols = rows * piece
    mask_rows, tiles = 2 * mask_buf.shape[1], mask_buf.shape[2]
    arrived(first.at[twin], first_sem.at[twin])
    for other in others_chip:
        for k in range(2):
            arrived(first.at[2 * other + k], first_sem.at[2 * other + k])
    line = first[:, piece:, :128].reshape(rows * AUX, 128)[:, :piece]
    at = iota((piece, n_cols), 1)
    spread = dot(line, (iota((piece, n_cols), 0) == lax.rem(at, piece)).astype(jnp.float32))
    at = iota((rows * AUX, n_cols), 1)
    keep = iota((rows * AUX, n_cols), 0) == (at // piece) * AUX
    col_sharp = jnp.sum(jnp.where(keep, spread, 0.0), axis=0, keepdims=True)
    labels = jnp.concatenate(split(first[:, :piece].reshape(n_cols, half)), axis=1)

    arrived(mask_buf.at[1 - core], mask_sem)
    wanted = (iota((tiles, n_cols), 1) // piece) * cols + z
    pick_cols = (iota((tiles, n_cols), 0) == wanted).astype(jnp.bfloat16)
    col_mask = quick(mask_buf[...].reshape(mask_rows, tiles).astype(jnp.bfloat16), pick_cols)
    col_mask = col_mask.astype(jnp.bfloat16)

    arrived(row_aux.at[2 * z + 1 - core], aux_sem.at[2 * z + 1 - core])
    for other in others_z:
        for k in range(2):
            arrived(row_aux.at[2 * other + k], aux_sem.at[2 * other + k])

    arrived(col_emb.at[twin], col_sem.at[twin])
    for other in others_chip:
        slot = 2 * other + 1 - core
        arrived(col_emb.at[slot], col_sem.at[slot])
    theirs = col_emb[...].reshape(n_cols, width)
    c_high[...], c_low[...] = split(theirs)
    col_squares = dot(jnp.ones((8, width), jnp.float32), theirs * theirs, 1, 1)[:1]

    def product(c, labels):
        wide = quick(w_high[c], labels)
        return wide[:, :half] + wide[:, half:] + quick(w_low[c], labels[:, :half])

    def block(c):
        ours = row_emb[pl.ds(2 * c, 2)].reshape(pair, width)
        both = jnp.concatenate(split(ours), axis=0)
        by_high, by_low = quick(both, c_high[...], 1), quick(both, c_low[...], 1)
        cross = by_high[:pair] + (by_high[pair:] + by_low[:pair] + by_low[pair:])
        squares = jnp.sum(ours * ours, axis=1, keepdims=True)
        sharp_at = row_aux[pl.ds(2 * c, 2)]
        row_sharp = jnp.concatenate([to_column(sharp_at[g, :1, :piece]) for g in range(2)], axis=0)
        wanted = (iota((pair, mask_rows), 0) // piece) * (mask_rows // 2) + c
        pick = (iota((pair, mask_rows), 1) == wanted).astype(jnp.bfloat16)
        distance = squares + col_squares - 2.0 * cross
        value = jnp.exp(-(distance * row_sharp * col_sharp)) * quick(pick, col_mask)
        w_high[c], w_low[c] = split(value)
        part[0, c, :pair] = product(c, labels)
        sums = to_line(jnp.sum(value, axis=1, keepdims=True))
        part[0, c, pair:, :pair] = jnp.broadcast_to(sums, (AUX, pair))

    def send_part(step, other, depth):
        push(
            part.at[step, other, pl.ds(0, depth)], summed.at[step, z, pl.ds(0, depth)],
            sum_sem.at[step, z], (r, other),
        )

    if others_z:
        hand_on(others_z[0])
    arrived(row_emb.at[2 * z + 1 - core], row_sem.at[2 * z + 1 - core])
    block(z)
    for i, other in enumerate(others_z):
        if i + 1 < len(others_z):
            hand_on(others_z[i + 1])
        slot = 2 * other + 1 - core
        arrived(row_emb.at[slot], row_sem.at[slot])
        block(other)
        send_part(0, other, pair + AUX)

    kept = jnp.concatenate([first[2 * chip, :piece], first[2 * chip + 1, :piece]], axis=0)
    kept = 0.1 * kept
    scale = None
    for step in range(ITERS):
        if step > 0:
            labels = jnp.concatenate(split(later[step - 1].reshape(n_cols, half)), axis=1)
        if step < ITERS - 1:
            depth = pair + AUX if step == 0 else pair
            if step > 0:
                for other in reversed(others_z):
                    part[step, other, :pair] = product(other, labels)
                    send_part(step, other, depth)
                part[step, z, :pair] = product(z, labels)
            total = part[step, z, :depth]
            for other in others_z:
                arrived(summed.at[step, other, pl.ds(0, depth)], sum_sem.at[step, other])
                total = total + summed[step, other, :depth]
            if step == 0:
                scale = 0.9 / to_column(total[pair : pair + 1, :pair])
            later[step, chip] = total[:pair] * scale + kept
            for other in reversed(others_chip):
                push(
                    later.at[step, chip], later.at[step, chip], later_sem.at[step, chip],
                    (2 * other + core, z),
                )
            for other in others_chip:
                arrived(later.at[step, other], later_sem.at[step, other])
        else:
            for other in reversed(others_z):
                last_part[other] = product(other, labels).reshape(2, piece, half)
                for k in range(2):
                    push(last_part.at[other, k], last.at[z, core], last_sem.at[z, core], (2 * chip + k, other))
            last_part[z] = product(z, labels).reshape(2, piece, half)
            push(last_part.at[z, 1 - core], last.at[z, core], last_sem.at[z, core], (twin, z))
            last[z, core] = last_part[z, core]
            arrived(last.at[z, 1 - core], last_sem.at[z, 1 - core])
            for other in others_z:
                for k in range(2):
                    arrived(last.at[other, k], last_sem.at[other, k])
            total = jnp.sum(last[...], axis=0)
            own = jnp.where(core == 0, scale[:piece], scale[piece:])
            for k in range(2):
                out_ref[:, k * half : (k + 1) * half] = total[k] * own + 0.1 * send[k, :piece]
    for copy in sent:
        copy.wait_send()


def round_up(n, m):
    return (n + m - 1) // m * m


def local(chips, cols, embeddings, sharpness, soft_labels, seed_mask, tile_mask):
    piece, width = embeddings.shape
    half = soft_labels.shape[1] // 2
    rows = 2 * chips
    tile_rows, tiles = round_up(tile_mask.shape[0], 8), round_up(tile_mask.shape[1], 128)
    pair = 2 * piece
    sends = (
        2 * (cols - 1) + 2 * (chips - 1) + 2 + 1 + 2 * (cols - 1) + 1 + 2 * (chips - 1) + 1
        + (ITERS - 1) * (cols + chips - 2) + 2 * cols - 1
    )
    f32, bf16, dma = jnp.float32, jnp.bfloat16, pltpu.SemaphoreType.DMA
    vmem = pl.BlockSpec(memory_space=pltpu.VMEM)
    return pl.pallas_call(
        functools.partial(kernel, chips, cols),
        out_shape=jax.ShapeDtypeStruct(soft_labels.shape, f32),
        in_specs=[pl.BlockSpec(memory_space=pltpu.HBM)] * 5,
        out_specs=vmem,
        scratch_shapes=[
            pltpu.VMEM((2 * cols, piece, width), f32),
            pltpu.VMEM((rows, piece, width), f32),
            pltpu.VMEM((2 * cols, AUX, 128), f32),
            pltpu.VMEM((2, tile_rows, tiles), f32),
            pltpu.VMEM((rows, piece + AUX, half), f32),
            pltpu.VMEM((ITERS - 1, chips, pair, half), f32),
            pltpu.VMEM((ITERS - 1, cols, pair + AUX, half), f32),
            pltpu.VMEM((ITERS - 1, cols, pair + AUX, half), f32),
            pltpu.VMEM((cols, 2, piece, half), f32),
            pltpu.VMEM((cols, 2, piece, half), f32),
            pltpu.VMEM((cols, pair, rows * piece), bf16),
            pltpu.VMEM((cols, pair, rows * piece), bf16),
            pltpu.VMEM((rows * piece, width), bf16),
            pltpu.VMEM((rows * piece, width), bf16),
            pltpu.VMEM((2, piece + AUX, half), f32),
            pltpu.VMEM(soft_labels.shape, f32),
            pltpu.VMEM((1, piece), f32),
            pltpu.VMEM((1, piece), jnp.int32),
            pltpu.VMEM(tile_mask.shape, jnp.int32),
            dma((2 * cols,)),
            dma((rows,)),
            dma((2 * cols,)),
            dma(()),
            dma((rows,)),
            dma((ITERS - 1, chips)),
            dma((ITERS - 1, cols)),
            dma((cols, 2)),
            dma((sends,)),
            dma((6,)),
        ],
        compiler_params=pltpu.CompilerParams(
            collective_id=0, has_side_effects=True, vmem_limit_bytes=48 * 1024 * 1024
        ),
    )(embeddings, sharpness.reshape(1, piece), soft_labels, seed_mask.reshape(1, piece), tile_mask)


def solution(mesh):
    return jax.shard_map(
        functools.partial(local, mesh.shape["row"] // 2, mesh.shape["col"]),
        mesh=mesh,
        in_specs=(
            P(("row", "col"), None),
            P(("row", "col")),
            P(("row", "col"), None),
            P(("row", "col")),
            P("row", None),
        ),
        out_specs=P(("row", "col"), None),
        check_vma=False,
    )
```

time: 45.1 us -> 46.2 us (1.024)
  Pallas kernels: 41.9 us -> 43 us
    pallas_call x1, Pallas kernels: 41.9 us -> 43 us  [local(): pl.pallas_call(functools.partial(kernel, chips, cols), out_shape=jax.Shap...]
where the time goes in v2:
time: 46.2 us; the launch traced here: 45.9 us
  Pallas kernels  43 us (93%)
  local copies, waits for them, and re-layouts  2.95 us (6%)
    pallas_call x1, Pallas kernels, local(): pl.pallas_call(functools.partial(kernel, chips, cols), out_shape=jax.Shap...  43 us
    unnamed x11, local copies, waits for them, and re-layouts  2.95 us

profile of v2, /device:TPU:0, one launch (start us, length us, event | category | flops | bytes accessed | tf_op | source)
XLA Modules:
  0.0 45.9 jit_solution(7656021880138572634)
XLA Ops:
  0.0 0.0 copy-start.2
  0.0 0.0 copy-start.3
  0.0 0.0 copy-start.4
  0.0 0.7 %copy-done.2 = s32[4,32]{1,0:T(4,128)S(1)} copy-done((s32[4,32]{1,0:T(4,128)S(1)}, s32[4,32]{1,0:T(4,128)}, u32[]{:S(2)}) %copy-start.2) | copy-done | bytes 536
  0.7 0.0 copy-done.3
  0.7 0.0 copy-done.4
  0.7 0.0 copy-start
  0.7 0.9 %copy-done = f32[32,768]{1,0:T(8,128)S(1)} copy-done((f32[32,768]{1,0:T(8,128)S(1)}, f32[32,768]{1,0:T(8,128)}, u32[]{:S(2)}) %copy-start) | copy-done | bytes 98328
  1.6 0.0 copy-start.1
  1.6 0.8 %copy-done.1 = f32[32,256]{1,0:T(8,128)S(1)} copy-done((f32[32,256]{1,0:T(8,128)S(1)}, f32[32,256]{1,0:T(8,128)}, u32[]{:S(2)}) %copy-start.1) | copy-done | bytes 32792
  2.3 43.0 %shard_map.55 = f32[32,256]{1,0:T(8,128)S(1)} custom-call(f32[32,768]{1,0:T(8,128)S(1)} %copy-done, f32[1,32]{1,0:T(1,128)S(1)} %bitcast.2, f32[32,256]{1,0:T(8,128)S(1)} %copy-done.1, s32[1,32]{1,0:T(1,128)S(1)} %bitcast.3, s32[4,32]{1,0:T(4,128)S(1)} %copy-done.2), custom_call_target="tpu_custom_call" | custom-call | tf_op jit(solution)/shard_map/pallas_call | solution.py:275
  45.3 0.6 %copy.7 = f32[32,256]{1,0:T(8,128)} copy(f32[32,256]{1,0:T(8,128)S(1)} %shard_map.55) | data formatting | bytes 65536
Async XLA Ops:
  0.0 0.7 %copy-start.2 = (s32[4,32]{1,0:T(4,128)S(1)}, s32[4,32]{1,0:T(4,128)}, u32[]{:S(2)}) copy-start(s32[4,32]{1,0:T(4,128)} %tile_ref.1) | copy-start | bytes 1540
  0.0 0.7 %copy-start.3 = (f32[32]{0:T(128)S(1)}, f32[32]{0:T(128)}, u32[]{:S(2)}) copy-start(f32[32]{0:T(128)} %param.6) | copy-start | bytes 388
  0.0 0.7 %copy-start.4 = (s32[32]{0:T(128)S(1)}, s32[32]{0:T(128)}, u32[]{:S(2)}) copy-start(s32[32]{0:T(128)} %param.8) | copy-start | bytes 388
  0.7 0.9 %copy-start = (f32[32,768]{1,0:T(8,128)S(1)}, f32[32,768]{1,0:T(8,128)}, u32[]{:S(2)}) copy-start(f32[32,768]{1,0:T(8,128)} %emb_ref.1) | copy-start | bytes 294916
  1.6 0.8 %copy-start.1 = (f32[32,256]{1,0:T(8,128)S(1)}, f32[32,256]{1,0:T(8,128)}, u32[]{:S(2)}) copy-start(f32[32,256]{1,0:T(8,128)} %soft_ref.1) | copy-start | bytes 98308

commit v3 on v2

--- a/solution.py
+++ b/solution.py
@@ -50,9 +50,9 @@
 
 def kernel(
     chips, cols, emb_ref, sharp_ref, soft_ref, seed_ref, tile_ref, out_ref,
-    row_emb, col_emb, row_aux, mask_buf, first, later, part, summed, last_part, last,
+    row_emb, col_emb, row_aux, mask_buf, col_mask, first, tiles, later, part, summed, last_part, last,
     w_high, w_low, c_high, c_low, send, soft, sharp_in, seed_in, tile_in,
-    row_sem, col_sem, aux_sem, mask_sem, first_sem, later_sem, sum_sem, last_sem, send_sem, load_sem,
+    row_sem, col_sem, aux_sem, tile_sem, first_sem, later_sem, sum_sem, last_sem, send_sem, load_sem,
 ):
     piece, width = emb_ref.shape
     half = soft_ref.shape[1] // 2
@@ -61,7 +61,6 @@
     r, z = lax.axis_index("row"), lax.axis_index("col")
     chip, core = r // 2, lax.rem(r, 2)
     twin = r + 1 - 2 * core
-    mine = 2 * z + core
 
     others_z = [lax.rem(z + d, cols) for d in by_distance(cols)]
     others_chip = [lax.rem(chip + d, chips) for d in by_distance(chips)]
@@ -69,32 +68,16 @@
     peers += [(2 * chip + k, other) for other in others_z for k in range(2)]
     peers += [(2 * other + k, z) for other in others_chip for k in range(2)]
 
+    barrier = pltpu.get_barrier_semaphore()
+    for peer in peers:
+        pl.semaphore_signal(barrier, inc=1, device_id=peer, device_id_type=MESH)
     loads = []
     for src, dst in (
-        (emb_ref, row_emb.at[mine]), (soft_ref, soft), (sharp_ref, sharp_in), (seed_ref, seed_in),
-        (tile_ref, tile_in), (emb_ref, col_emb.at[r]),
+        (emb_ref, row_emb.at[z]), (emb_ref, col_emb.at[r]), (soft_ref, soft), (sharp_ref, sharp_in),
+        (seed_ref, seed_in), (tile_ref, tile_in),
     ):
         loads.append(pltpu.make_async_copy(src, dst, load_sem.at[len(loads)]))
         loads[-1].start()
-    barrier = pltpu.get_barrier_semaphore()
-    for peer in peers:
-        pl.semaphore_signal(barrier, inc=1, device_id=peer, device_id_type=MESH)
-    mask_buf[core] = jnp.zeros(mask_buf.shape[1:], jnp.float32)
-    for load in loads:
-        load.wait()
-
-    sharp = sharp_in[...]
-    aux = jnp.concatenate([sharp, jnp.zeros((1, 128 - piece), jnp.float32)], axis=1)
-    aux = jnp.broadcast_to(aux, (AUX, 128))
-    row_aux[mine] = aux
-    mask_buf[core, : tile_ref.shape[0], : tile_ref.shape[1]] = tile_in[...].astype(jnp.float32)
-    seeded = to_column(seed_in[...].astype(jnp.float32)) * soft[...]
-    for k in range(2):
-        send[k, :piece] = seeded[:, k * half : (k + 1) * half]
-        send[k, piece:, :128] = aux
-    first[r] = send[core]
-    pl.semaphore_wait(barrier, len(peers))
-
     sent = []
 
     def push(src, dst, recv, peer):
@@ -111,34 +94,52 @@
             device_id=(twin, z), device_id_type=MESH,
         ).wait_recv()
 
+    for load in loads:
+        load.wait()
+    aux = jnp.concatenate([sharp_in[...], jnp.zeros((1, 128 - piece), jnp.float32)], axis=1)
+    aux = jnp.broadcast_to(aux, (AUX, 128))
+    row_aux[z] = aux
+    seeded = to_column(seed_in[...].astype(jnp.float32)) * soft[...]
+    for k in range(2):
+        send[k, :piece] = seeded[:, k * half : (k + 1) * half]
+        send[k, piece:, :128] = aux
+    first[r] = send[core]
+    pl.semaphore_wait(barrier, len(peers))
+
     for other in others_z:
-        push(row_emb.at[mine], row_emb.at[mine], row_sem.at[mine], (r, other))
+        push(row_emb.at[z], row_emb.at[z], row_sem.at[z], (r, other))
     for other in others_chip:
         push(col_emb.at[r], col_emb.at[r], col_sem.at[r], (2 * other + core, z))
     push(col_emb.at[r], col_emb.at[r], col_sem.at[r], (twin, z))
-    push(row_emb.at[mine], row_emb.at[mine], row_sem.at[mine], (twin, z))
     for other in others_chip:
         for k in range(2):
             push(send.at[k], first.at[r], first_sem.at[r], (2 * other + k, z))
     push(send.at[1 - core], first.at[r], first_sem.at[r], (twin, z))
-    push(mask_buf.at[core], mask_buf.at[core], mask_sem, (twin, z))
-    push(row_aux.at[mine], row_aux.at[mine], aux_sem.at[mine], (twin, z))
     for other in others_z:
-        for k in range(2):
-            push(row_aux.at[mine], row_aux.at[mine], aux_sem.at[mine], (2 * chip + k, other))
+        push(row_aux.at[z], row_aux.at[z], aux_sem.at[z], (r, other))
+
+    n_cols = rows * piece
+    n_tiles = mask_buf.shape[1]
+    mask_buf[...] = jnp.zeros(mask_buf.shape, jnp.float32)
+    mask_buf[: tile_ref.shape[0], : tile_ref.shape[1]] = tile_in[...].astype(jnp.float32)
+    wanted = (iota((n_tiles, n_cols), 1) // piece) * cols + z
+    pick_cols = (iota((n_tiles, n_cols), 0) == wanted).astype(jnp.bfloat16)
+    col_mask[...] = quick(mask_buf[...].astype(jnp.bfloat16), pick_cols)
 
     for other in others_chip:
         slot = 2 * other + core
         arrived(col_emb.at[slot], col_sem.at[slot])
         push(col_emb.at[slot], col_emb.at[slot], col_sem.at[slot], (twin, z))
 
-    def hand_on(other):
-        slot = 2 * other + core
-        arrived(row_emb.at[slot], row_sem.at[slot])
-        push(row_emb.at[slot], row_emb.at[slot], row_sem.at[slot], (twin, z))
-
-    n_cols = rows * piece
-    mask_rows, tiles = 2 * mask_buf.shape[1], mask_buf.shape[2]
+    def take(slot):
+        theirs = col_emb[slot]
+        at = pl.ds(pl.multiple_of(slot * piece, piece), piece)
+        c_high[at], c_low[at] = split(theirs)
+
+    take(r)
+    for other in others_chip:
+        take(2 * other + core)
+
     arrived(first.at[twin], first_sem.at[twin])
     for other in others_chip:
         for k in range(2):
@@ -151,23 +152,13 @@
     col_sharp = jnp.sum(jnp.where(keep, spread, 0.0), axis=0, keepdims=True)
     labels = jnp.concatenate(split(first[:, :piece].reshape(n_cols, half)), axis=1)
 
-    arrived(mask_buf.at[1 - core], mask_sem)
-    wanted = (iota((tiles, n_cols), 1) // piece) * cols + z
-    pick_cols = (iota((tiles, n_cols), 0) == wanted).astype(jnp.bfloat16)
-    col_mask = quick(mask_buf[...].reshape(mask_rows, tiles).astype(jnp.bfloat16), pick_cols)
-    col_mask = col_mask.astype(jnp.bfloat16)
-
-    arrived(row_aux.at[2 * z + 1 - core], aux_sem.at[2 * z + 1 - core])
-    for other in others_z:
-        for k in range(2):
-            arrived(row_aux.at[2 * other + k], aux_sem.at[2 * other + k])
-
     arrived(col_emb.at[twin], col_sem.at[twin])
+    take(twin)
     for other in others_chip:
         slot = 2 * other + 1 - core
         arrived(col_emb.at[slot], col_sem.at[slot])
+        take(slot)
     theirs = col_emb[...].reshape(n_cols, width)
-    c_high[...], c_low[...] = split(theirs)
     col_squares = dot(jnp.ones((8, width), jnp.float32), theirs * theirs, 1, 1)[:1]
 
     def product(c, labels):
@@ -175,17 +166,20 @@
         return wide[:, :half] + wide[:, half:] + quick(w_low[c], labels[:, :half])
 
     def block(c):
-        ours = row_emb[pl.ds(2 * c, 2)].reshape(pair, width)
+        ours = row_emb[c]
         both = jnp.concatenate(split(ours), axis=0)
         by_high, by_low = quick(both, c_high[...], 1), quick(both, c_low[...], 1)
-        cross = by_high[:pair] + (by_high[pair:] + by_low[:pair] + by_low[pair:])
+        cross = by_high[:piece] + (by_high[piece:] + by_low[:piece] + by_low[piece:])
         squares = jnp.sum(ours * ours, axis=1, keepdims=True)
-        sharp_at = row_aux[pl.ds(2 * c, 2)]
-        row_sharp = jnp.concatenate([to_column(sharp_at[g, :1, :piece]) for g in range(2)], axis=0)
-        wanted = (iota((pair, mask_rows), 0) // piece) * (mask_rows // 2) + c
-        pick = (iota((pair, mask_rows), 1) == wanted).astype(jnp.bfloat16)
+        row_sharp = to_column(row_aux[c][:1, :piece])
         distance = squares + col_squares - 2.0 * cross
-        value = jnp.exp(-(distance * row_sharp * col_sharp)) * quick(pick, col_mask)
+        value = jnp.exp(-(distance * row_sharp * col_sharp)) * col_mask[pl.ds(c, 1)]
+        tiles[c, core] = value
+        push(tiles.at[c, core], tiles.at[c, core], tile_sem.at[c], (twin, z))
+
+    def finish(c):
+        arrived(tiles.at[c, 1 - core], tile_sem.at[c])
+        value = tiles[c].reshape(pair, n_cols)
         w_high[c], w_low[c] = split(value)
         part[0, c, :pair] = product(c, labels)
         sums = to_line(jnp.sum(value, axis=1, keepdims=True))
@@ -197,17 +191,20 @@
             sum_sem.at[step, z], (r, other),
         )
 
-    if others_z:
-        hand_on(others_z[0])
-    arrived(row_emb.at[2 * z + 1 - core], row_sem.at[2 * z + 1 - core])
     block(z)
     for i, other in enumerate(others_z):
-        if i + 1 < len(others_z):
-            hand_on(others_z[i + 1])
-        slot = 2 * other + 1 - core
-        arrived(row_emb.at[slot], row_sem.at[slot])
+        arrived(row_aux.at[other], aux_sem.at[other])
+        arrived(row_emb.at[other], row_sem.at[other])
         block(other)
-        send_part(0, other, pair + AUX)
+        before = others_z[i - 1] if i else z
+        finish(before)
+        if i:
+            send_part(0, before, pair + AUX)
+    if others_z:
+        finish(others_z[-1])
+        send_part(0, others_z[-1], pair + AUX)
+    else:
+        finish(z)
 
     kept = jnp.concatenate([first[2 * chip, :piece], first[2 * chip + 1, :piece]], axis=0)
     kept = 0.1 * kept
@@ -264,10 +261,10 @@
     piece, width = embeddings.shape
     half = soft_labels.shape[1] // 2
     rows = 2 * chips
-    tile_rows, tiles = round_up(tile_mask.shape[0], 8), round_up(tile_mask.shape[1], 128)
+    tile_rows, n_tiles = round_up(tile_mask.shape[0], 16), round_up(tile_mask.shape[1], 128)
     pair = 2 * piece
     sends = (
-        2 * (cols - 1) + 2 * (chips - 1) + 2 + 1 + 2 * (cols - 1) + 1 + 2 * (chips - 1) + 1
+        (cols - 1) + (chips - 1) + 1 + 2 * (chips - 1) + 1 + (cols - 1) + (chips - 1) + cols
         + (ITERS - 1) * (cols + chips - 2) + 2 * cols - 1
     )
     f32, bf16, dma = jnp.float32, jnp.bfloat16, pltpu.SemaphoreType.DMA
@@ -278,11 +275,13 @@
         in_specs=[pl.BlockSpec(memory_space=pltpu.HBM)] * 5,
         out_specs=vmem,
         scratch_shapes=[
-            pltpu.VMEM((2 * cols, piece, width), f32),
+            pltpu.VMEM((cols, piece, width), f32),
             pltpu.VMEM((rows, piece, width), f32),
-            pltpu.VMEM((2 * cols, AUX, 128), f32),
-            pltpu.VMEM((2, tile_rows, tiles), f32),
+            pltpu.VMEM((cols, AUX, 128), f32),
+            pltpu.VMEM((tile_rows, n_tiles), f32),
+            pltpu.VMEM((tile_rows, rows * piece), f32),
             pltpu.VMEM((rows, piece + AUX, half), f32),
+            pltpu.VMEM((cols, 2, piece, rows * piece), f32),
             pltpu.VMEM((ITERS - 1, chips, pair, half), f32),
             pltpu.VMEM((ITERS - 1, cols, pair + AUX, half), f32),
             pltpu.VMEM((ITERS - 1, cols, pair + AUX, half), f32),
@@ -297,10 +296,10 @@
             pltpu.VMEM((1, piece), f32),
             pltpu.VMEM((1, piece), jnp.int32),
             pltpu.VMEM(tile_mask.shape, jnp.int32),
-            dma((2 * cols,)),
+            dma((cols,)),
             dma((rows,)),
-            dma((2 * cols,)),
-            dma(()),
+            dma((cols,)),
+            dma((cols,)),
             dma((rows,)),
             dma((ITERS - 1, chips)),
             dma((ITERS - 1, cols)),
@@ -309,7 +308,7 @@
             dma((6,)),
         ],
         compiler_params=pltpu.CompilerParams(
-            collective_id=0, has_side_effects=True, vmem_limit_bytes=48 * 1024 * 1024
+            collective_id=0, has_side_effects=True, vmem_limit_bytes=60 * 1024 * 1024
         ),
     )(embeddings, sharpness.reshape(1, piece), soft_labels, seed_mask.reshape(1, piece), tile_mask)
 

time: 46.2 us -> 42.3 us (0.916)
  Pallas kernels: 43 us -> 40.7 us
  local copies, waits for them, and re-layouts: 2.95 us -> 1.38 us
    pallas_call x1, Pallas kernels: 43 us -> 40.7 us  [local(): pl.pallas_call(functools.partial(kernel, chips, cols), out_shape=jax.Shap...]
    unnamed x11 -> x1, local copies, waits for them, and re-layouts: 2.95 us -> 1.38 us
where the time goes in v3:
time: 42.3 us; the launch traced here: 42.1 us
  Pallas kernels  40.7 us (96%)
  local copies, waits for them, and re-layouts  1.38 us (3%)
    pallas_call x1, Pallas kernels, local(): pl.pallas_call(functools.partial(kernel, chips, cols), out_shape=jax.Shap...  40.7 us
    unnamed x1, local copies, waits for them, and re-layouts  1.38 us

profile of v3, /device:TPU:0, one launch (start us, length us, event | category | flops | bytes accessed | tf_op | source)
XLA Modules:
  0.0 42.1 jit_solution(8628105114486240191)
XLA Ops:
  0.0 40.7 %shard_map.55 = f32[32,256]{1,0:T(8,128)} custom-call(f32[32,768]{1,0:T(8,128)} %emb_ref.1, f32[1,32]{1,0:T(1,128)} %bitcast.2, f32[32,256]{1,0:T(8,128)} %soft_ref.1, s32[1,32]{1,0:T(1,128)} %bitcast.3, s32[4,32]{1,0:T(4,128)} %tile_ref.1), custom_call_target="tpu_custom_call" | custom-call | tf_op jit(solution)/shard_map/pallas_call | solution.py:272
  40.7 1.4 %copy.7 = f32[32,256]{1,0:T(8,128)} copy(f32[32,256]{1,0:T(8,128)} %shard_map.55) | data formatting | bytes 65536

commit v4 on v3

v4 whole, which is shorter than its diff:
```python
import functools

import jax
import jax.numpy as jnp
from jax import lax
from jax.experimental import pallas as pl
from jax.experimental.pallas import tpu as pltpu
from jax.sharding import PartitionSpec as P

ITERS = 3
MESH = pl.DeviceIdType.MESH
EXACT = lax.Precision.HIGHEST
AUX = 8


def dot(a, b, a_dim=1, b_dim=0):
    return lax.dot_general(
        a, b, (((a_dim,), (b_dim,)), ((), ())), precision=EXACT, preferred_element_type=jnp.float32
    )


def iota(shape, dim):
    return lax.broadcasted_iota(jnp.int32, shape, dim)


def to_column(line):
    n = line.shape[1]
    eye = iota((n, n), 0) == iota((n, n), 1)
    return jnp.sum(jnp.where(eye, jnp.broadcast_to(line, (n, n)), 0.0), axis=1, keepdims=True)


def to_line(column):
    n = column.shape[0]
    eye = iota((n, n), 0) == iota((n, n), 1)
    return jnp.sum(jnp.where(eye, jnp.broadcast_to(column, (n, n)), 0.0), axis=0, keepdims=True)


def split(value):
    high = value.astype(jnp.bfloat16)
    return high, (value - high.astype(jnp.float32)).astype(jnp.bfloat16)


def quick(a, b, b_dim=0):
    return lax.dot_general(a, b, (((1,), (b_dim,)), ((), ())), preferred_element_type=jnp.float32)


def by_distance(n):
    return sorted(range(1, n), key=lambda d: (min(d, n - d), d))


def kernel(
    chips, cols, emb_ref, sharp_ref, soft_ref, seed_ref, tile_ref, out_ref,
    row_emb, col_buf, row_aux, mask_buf, col_mask, tiles, part, summed, new_labels, later,
    next_part, next_sum, last_labels, last_part, last,
    w_high, w_low, c_high, c_low, soft, sharp_in, seed_in, tile_in,
    row_sem, col_sem, aux_sem, tile_sem, later_sem, sum_sem, last_label_sem, next_sum_sem, last_sem,
    send_sem, load_sem,
):
    piece, width = emb_ref.shape
    n_labels = soft_ref.shape[1]
    half = n_labels // 2
    rows = 2 * chips
    pair = 2 * piece
    end = width + n_labels
    r, z = lax.axis_index("row"), lax.axis_index("col")
    chip, core = r // 2, lax.rem(r, 2)
    twin = r + 1 - 2 * core

    others_z = [lax.rem(z + d, cols) for d in by_distance(cols)]
    others_chip = [lax.rem(chip + d, chips) for d in by_distance(chips)]
    peers = [(twin, z)]
    peers += [(2 * chip + k, other) for other in others_z for k in range(2)]
    peers += [(2 * other + k, z) for other in others_chip for k in range(2)]

    barrier = pltpu.get_barrier_semaphore()
    for peer in peers:
        pl.semaphore_signal(barrier, inc=1, device_id=peer, device_id_type=MESH)
    loads = []
    for src, dst in (
        (emb_ref, row_emb.at[z]), (emb_ref, col_buf.at[r, :, pl.ds(0, width)]), (soft_ref, soft),
        (sharp_ref, sharp_in), (seed_ref, seed_in), (tile_ref, tile_in),
    ):
        loads.append(pltpu.make_async_copy(src, dst, load_sem.at[len(loads)]))
        loads[-1].start()
    sent = []

    def push(src, dst, recv, peer):
        copy = pltpu.make_async_remote_copy(
            src_ref=src, dst_ref=dst, send_sem=send_sem.at[len(sent)], recv_sem=recv,
            device_id=peer, device_id_type=MESH,
        )
        copy.start()
        sent.append(copy)

    def arrived(dst, recv):
        pltpu.make_async_remote_copy(
            src_ref=dst, dst_ref=dst, send_sem=send_sem.at[0], recv_sem=recv,
            device_id=(twin, z), device_id_type=MESH,
        ).wait_recv()

    for load in loads:
        load.wait()
    aux = jnp.concatenate([sharp_in[...], jnp.zeros((1, 128 - piece), jnp.float32)], axis=1)
    row_aux[z] = jnp.broadcast_to(aux, (AUX, 128))
    col_buf[r, :, end:] = jnp.broadcast_to(aux, (piece, 128))
    seeded = to_column(seed_in[...].astype(jnp.float32)) * soft[...]
    col_buf[r, :, width:end] = seeded
    pl.semaphore_wait(barrier, len(peers))

    for other in others_z:
        push(row_emb.at[z], row_emb.at[z], row_sem.at[z], (r, other))
    for other in others_chip:
        push(col_buf.at[r], col_buf.at[r], col_sem.at[r], (2 * other + core, z))
    push(col_buf.at[r], col_buf.at[r], col_sem.at[r], (twin, z))
    for other in others_z:
        push(row_aux.at[z], row_aux.at[z], aux_sem.at[z], (r, other))

    n_cols = rows * piece
    n_tiles = mask_buf.shape[1]
    mask_buf[...] = jnp.zeros(mask_buf.shape, jnp.float32)
    mask_buf[: tile_ref.shape[0], : tile_ref.shape[1]] = tile_in[...].astype(jnp.float32)
    wanted = (iota((n_tiles, n_cols), 1) // piece) * cols + z
    pick_cols = (iota((n_tiles, n_cols), 0) == wanted).astype(jnp.bfloat16)
    col_mask[...] = quick(mask_buf[...].astype(jnp.bfloat16), pick_cols)

    def take(slot):
        at = pl.ds(pl.multiple_of(slot * piece, piece), piece)
        c_high[at], c_low[at] = split(col_buf[slot, :, :width])

    take(r)
    for other in others_chip:
        slot = 2 * other + core
        arrived(col_buf.at[slot], col_sem.at[slot])
        push(col_buf.at[slot], col_buf.at[slot], col_sem.at[slot], (twin, z))
    for other in others_chip:
        take(2 * other + core)
    arrived(col_buf.at[twin], col_sem.at[twin])
    take(twin)
    for other in others_chip:
        slot = 2 * other + 1 - core
        arrived(col_buf.at[slot], col_sem.at[slot])
        take(slot)
    theirs = col_buf[:, :, :width].reshape(n_cols, width)
    col_squares = dot(jnp.ones((8, width), jnp.float32), theirs * theirs, 1, 1)[:1]
    line = col_buf[:, :AUX, end:].reshape(rows * AUX, 128)[:, :piece]
    at = iota((piece, n_cols), 1)
    spread = dot(line, (iota((piece, n_cols), 0) == lax.rem(at, piece)).astype(jnp.float32))
    at = iota((rows * AUX, n_cols), 1)
    keep = iota((rows * AUX, n_cols), 0) == (at // piece) * AUX
    col_sharp = jnp.sum(jnp.where(keep, spread, 0.0), axis=0, keepdims=True)
    labels = jnp.concatenate(split(col_buf[:, :, width:end].reshape(n_cols, n_labels)), axis=1)

    def block(c):
        ours = row_emb[c]
        both = jnp.concatenate(split(ours), axis=0)
        by_high, by_low = quick(both, c_high[...], 1), quick(both, c_low[...], 1)
        cross = by_high[:piece] + (by_high[piece:] + by_low[:piece] + by_low[piece:])
        squares = jnp.sum(ours * ours, axis=1, keepdims=True)
        row_sharp = to_column(row_aux[c][:1, :piece])
        distance = squares + col_squares - 2.0 * cross
        value = jnp.exp(-(distance * row_sharp * col_sharp)) * col_mask[pl.ds(c, 1)]
        tiles[c, core] = value
        wide = quick(jnp.concatenate(split(value), axis=0), labels)
        low = wide[piece:, :n_labels] + wide[piece:, n_labels:] + wide[:piece, n_labels:]
        part[c, :piece] = wide[:piece, :n_labels] + low
        sums = to_line(jnp.sum(value, axis=1, keepdims=True))
        part[c, piece:, :piece] = jnp.broadcast_to(sums, (AUX, piece))

    block(z)
    for other in others_z:
        arrived(row_aux.at[other], aux_sem.at[other])
        arrived(row_emb.at[other], row_sem.at[other])
        block(other)
        push(part.at[other], summed.at[z], sum_sem.at[z], (r, other))
    for other in [z] + others_z:
        push(tiles.at[other, core], tiles.at[other, core], tile_sem.at[other], (twin, z))

    total = part[z]
    for other in others_z:
        arrived(summed.at[other], sum_sem.at[other])
        total = total + summed[other]
    degree = total[piece : piece + 1, :piece]
    own_scale = 0.9 / to_column(degree)
    own_kept = 0.1 * col_buf[r, :, width:end]
    value = total[:piece] * own_scale + own_kept
    for k in range(2):
        new_labels[k, :piece] = value[:, k * half : (k + 1) * half]
        new_labels[k, piece:, :piece] = jnp.broadcast_to(degree, (AUX, piece))
    for other in others_chip:
        for k in range(2):
            push(new_labels.at[k], later.at[r], later_sem.at[r], (2 * other + k, z))
    push(new_labels.at[1 - core], later.at[r], later_sem.at[r], (twin, z))
    later[r] = new_labels[core]

    for c in [z] + others_z:
        arrived(tiles.at[c, 1 - core], tile_sem.at[c])
        w_high[c], w_low[c] = split(tiles[c].reshape(pair, n_cols))

    def product(c, labels):
        wide = quick(w_high[c], labels)
        return wide[:, :half] + wide[:, half:] + quick(w_low[c], labels[:, :half])

    arrived(later.at[twin], later_sem.at[twin])
    for other in others_chip:
        for k in range(2):
            slot = 2 * other + k
            arrived(later.at[slot], later_sem.at[slot])

    pieces = [2 * chip, 2 * chip + 1]
    kept = jnp.concatenate([col_buf[p, :, width:end] for p in pieces], axis=0)
    kept = 0.1 * jnp.where(core == 0, kept[:, :half], kept[:, half:])
    scale = jnp.concatenate([0.9 / to_column(later[p, piece : piece + 1, :piece]) for p in pieces], axis=0)
    labels = later[:, :piece].reshape(n_cols, half)
    for step in range(ITERS - 2):
        labels = jnp.concatenate(split(labels), axis=1)
        for other in reversed(others_z):
            next_part[step, other] = product(other, labels)
            push(
                next_part.at[step, other], next_sum.at[step, z], next_sum_sem.at[step, z], (r, other)
            )
        total = product(z, labels)
        for other in others_z:
            arrived(next_sum.at[step, other], next_sum_sem.at[step, other])
            total = total + next_sum[step, other]
        last_labels[step, chip] = total * scale + kept
        for other in reversed(others_chip):
            push(
                last_labels.at[step, chip], last_labels.at[step, chip], last_label_sem.at[step, chip],
                (2 * other + core, z),
            )
        for other in others_chip:
            arrived(last_labels.at[step, other], last_label_sem.at[step, other])
        labels = last_labels[step].reshape(n_cols, half)

    labels = jnp.concatenate(split(labels), axis=1)
    for other in reversed(others_z):
        last_part[other] = product(other, labels).reshape(2, piece, half)
        for k in range(2):
            push(last_part.at[other, k], last.at[z, core], last_sem.at[z, core], (2 * chip + k, other))
    last_part[z] = product(z, labels).reshape(2, piece, half)
    push(last_part.at[z, 1 - core], last.at[z, core], last_sem.at[z, core], (twin, z))
    last[z, core] = last_part[z, core]
    arrived(last.at[z, 1 - core], last_sem.at[z, 1 - core])
    for other in others_z:
        for k in range(2):
            arrived(last.at[other, k], last_sem.at[other, k])
    total = jnp.sum(last[...], axis=0)
    for k in range(2):
        at = slice(k * half, (k + 1) * half)
        out_ref[:, at] = total[k] * own_scale + own_kept[:, at]
    for copy in sent:
        copy.wait_send()


def round_up(n, m):
    return (n + m - 1) // m * m


def local(chips, cols, embeddings, sharpness, soft_labels, seed_mask, tile_mask):
    piece, width = embeddings.shape
    half = soft_labels.shape[1] // 2
    rows = 2 * chips
    tile_rows, n_tiles = round_up(tile_mask.shape[0], 16), round_up(tile_mask.shape[1], 128)
    pair = 2 * piece
    n_cols = rows * piece
    middle = ITERS - 2
    sends = (
        2 * (cols - 1) + 2 * (chips - 1) + 1 + (cols - 1) + cols + 2 * (chips - 1) + 1
        + middle * (cols + chips - 2) + 2 * cols - 1
    )
    f32, bf16, dma = jnp.float32, jnp.bfloat16, pltpu.SemaphoreType.DMA
    vmem = pl.BlockSpec(memory_space=pltpu.VMEM)
    return pl.pallas_call(
        functools.partial(kernel, chips, cols),
        out_shape=jax.ShapeDtypeStruct(soft_labels.shape, f32),
        in_specs=[pl.BlockSpec(memory_space=pltpu.HBM)] * 5,
        out_specs=vmem,
        scratch_shapes=[
            pltpu.VMEM((cols, piece, width), f32),
            pltpu.VMEM((rows, piece, width + 2 * half + 128), f32),
            pltpu.VMEM((cols, AUX, 128), f32),
            pltpu.VMEM((tile_rows, n_tiles), f32),
            pltpu.VMEM((tile_rows, n_cols), f32),
            pltpu.VMEM((cols, 2, piece, n_cols), f32),
            pltpu.VMEM((cols, piece + AUX, 2 * half), f32),
            pltpu.VMEM((cols, piece + AUX, 2 * half), f32),
            pltpu.VMEM((2, piece + AUX, half), f32),
            pltpu.VMEM((rows, piece + AUX, half), f32),
            pltpu.VMEM((middle, cols, pair, half), f32),
            pltpu.VMEM((middle, cols, pair, half), f32),
            pltpu.VMEM((middle, chips, pair, half), f32),
            pltpu.VMEM((cols, 2, piece, half), f32),
            pltpu.VMEM((cols, 2, piece, half), f32),
            pltpu.VMEM((cols, pair, n_cols), bf16),
            pltpu.VMEM((cols, pair, n_cols), bf16),
            pltpu.VMEM((n_cols, width), bf16),
            pltpu.VMEM((n_cols, width), bf16),
            pltpu.VMEM(soft_labels.shape, f32),
            pltpu.VMEM((1, piece), f32),
            pltpu.VMEM((1, piece), jnp.int32),
            pltpu.VMEM(tile_mask.shape, jnp.int32),
            dma((cols,)),
            dma((rows,)),
            dma((cols,)),
            dma((cols,)),
            dma((rows,)),
            dma((cols,)),
            dma((middle, chips)),
            dma((middle, cols)),
            dma((cols, 2)),
            dma((sends,)),
            dma((6,)),
        ],
        compiler_params=pltpu.CompilerParams(
            collective_id=0, has_side_effects=True, vmem_limit_bytes=60 * 1024 * 1024
        ),
    )(embeddings, sharpness.reshape(1, piece), soft_labels, seed_mask.reshape(1, piece), tile_mask)


def solution(mesh):
    return jax.shard_map(
        functools.partial(local, mesh.shape["row"] // 2, mesh.shape["col"]),
        mesh=mesh,
        in_specs=(
            P(("row", "col"), None),
            P(("row", "col")),
            P(("row", "col"), None),
            P(("row", "col")),
            P("row", None),
        ),
        out_specs=P(("row", "col"), None),
        check_vma=False,
    )
```

time: 42.3 us -> 43.5 us (1.028)
  Pallas kernels: 40.7 us -> 41.9 us
    pallas_call x1, Pallas kernels: 40.7 us -> 41.9 us  [local(): pl.pallas_call(functools.partial(kernel, chips, cols), out_shape=jax.Shap...]
where the time goes in v4:
time: 43.5 us; the launch traced here: 43.3 us
  Pallas kernels  41.9 us (96%)
  local copies, waits for them, and re-layouts  1.38 us (3%)
    pallas_call x1, Pallas kernels, local(): pl.pallas_call(functools.partial(kernel, chips, cols), out_shape=jax.Shap...  41.9 us
    unnamed x1, local copies, waits for them, and re-layouts  1.38 us

profile of v4, /device:TPU:0, one launch (start us, length us, event | category | flops | bytes accessed | tf_op | source)
XLA Modules:
  0.0 43.3 jit_solution(8502112557327580213)
XLA Ops:
  0.0 41.9 %shard_map.55 = f32[32,256]{1,0:T(8,128)} custom-call(f32[32,768]{1,0:T(8,128)} %emb_ref.1, f32[1,32]{1,0:T(1,128)} %bitcast.2, f32[32,256]{1,0:T(8,128)} %soft_ref.1, s32[1,32]{1,0:T(1,128)} %bitcast.3, s32[4,32]{1,0:T(4,128)} %tile_ref.1), custom_call_target="tpu_custom_call" | custom-call | tf_op jit(solution)/shard_map/pallas_call | solution.py:273
  41.9 1.4 %copy.7 = f32[32,256]{1,0:T(8,128)} copy(f32[32,256]{1,0:T(8,128)} %shard_map.55) | data formatting | bytes 65536

commit v5 on v3

--- a/solution.py
+++ b/solution.py
@@ -96,8 +96,10 @@
 
     for load in loads:
         load.wait()
-    aux = jnp.concatenate([sharp_in[...], jnp.zeros((1, 128 - piece), jnp.float32)], axis=1)
-    aux = jnp.broadcast_to(aux, (AUX, 128))
+    held = row_emb[z]
+    norms = to_line(jnp.sum(held * held, axis=1, keepdims=True))
+    lines = jnp.where(iota((AUX, piece), 0) == 0, sharp_in[...], norms)
+    aux = jnp.concatenate([lines, jnp.zeros((AUX, 128 - piece), jnp.float32)], axis=1)
     row_aux[z] = aux
     seeded = to_column(seed_in[...].astype(jnp.float32)) * soft[...]
     for k in range(2):
@@ -106,11 +108,11 @@
     first[r] = send[core]
     pl.semaphore_wait(barrier, len(peers))
 
+    for other in reversed(others_chip):
+        push(col_emb.at[r], col_emb.at[r], col_sem.at[r], (2 * other + core, z))
+    push(col_emb.at[r], col_emb.at[r], col_sem.at[r], (twin, z))
     for other in others_z:
         push(row_emb.at[z], row_emb.at[z], row_sem.at[z], (r, other))
-    for other in others_chip:
-        push(col_emb.at[r], col_emb.at[r], col_sem.at[r], (2 * other + core, z))
-    push(col_emb.at[r], col_emb.at[r], col_sem.at[r], (twin, z))
     for other in others_chip:
         for k in range(2):
             push(send.at[k], first.at[r], first_sem.at[r], (2 * other + k, z))
@@ -150,6 +152,8 @@
     at = iota((rows * AUX, n_cols), 1)
     keep = iota((rows * AUX, n_cols), 0) == (at // piece) * AUX
     col_sharp = jnp.sum(jnp.where(keep, spread, 0.0), axis=0, keepdims=True)
+    keep = iota((rows * AUX, n_cols), 0) == (at // piece) * AUX + 1
+    col_squares = jnp.sum(jnp.where(keep, spread, 0.0), axis=0, keepdims=True)
     labels = jnp.concatenate(split(first[:, :piece].reshape(n_cols, half)), axis=1)
 
     arrived(col_emb.at[twin], col_sem.at[twin])
@@ -158,8 +162,6 @@
         slot = 2 * other + 1 - core
         arrived(col_emb.at[slot], col_sem.at[slot])
         take(slot)
-    theirs = col_emb[...].reshape(n_cols, width)
-    col_squares = dot(jnp.ones((8, width), jnp.float32), theirs * theirs, 1, 1)[:1]
 
     def product(c, labels):
         wide = quick(w_high[c], labels)
@@ -170,7 +172,7 @@
         both = jnp.concatenate(split(ours), axis=0)
         by_high, by_low = quick(both, c_high[...], 1), quick(both, c_low[...], 1)
         cross = by_high[:piece] + (by_high[piece:] + by_low[:piece] + by_low[piece:])
-        squares = jnp.sum(ours * ours, axis=1, keepdims=True)
+        squares = to_column(row_aux[c][1:2, :piece])
         row_sharp = to_column(row_aux[c][:1, :piece])
         distance = squares + col_squares - 2.0 * cross
         value = jnp.exp(-(distance * row_sharp * col_sharp)) * col_mask[pl.ds(c, 1)]

time: 42.3 us -> 42.3 us (level)
  no operation moved by 1% of the time
where the time goes in v5:
time: 42.3 us; the launch traced here: 42.1 us
  Pallas kernels  40.7 us (96%)
  local copies, waits for them, and re-layouts  1.38 us (3%)
    pallas_call x1, Pallas kernels, local(): pl.pallas_call(functools.partial(kernel, chips, cols), out_shape=jax.Shap...  40.7 us
    unnamed x1, local copies, waits for them, and re-layouts  1.38 us

profile of v5, /device:TPU:0, one launch (start us, length us, event | category | flops | bytes accessed | tf_op | source)
XLA Modules:
  0.0 42.1 jit_solution(5144836317283611202)
XLA Ops:
  0.0 40.7 %shard_map.55 = f32[32,256]{1,0:T(8,128)} custom-call(f32[32,768]{1,0:T(8,128)} %emb_ref.1, f32[1,32]{1,0:T(1,128)} %bitcast.2, f32[32,256]{1,0:T(8,128)} %soft_ref.1, s32[1,32]{1,0:T(1,128)} %bitcast.3, s32[4,32]{1,0:T(4,128)} %tile_ref.1), custom_call_target="tpu_custom_call" | custom-call | tf_op jit(solution)/shard_map/pallas_call | solution.py:274
  40.7 1.4 %copy.7 = f32[32,256]{1,0:T(8,128)} copy(f32[32,256]{1,0:T(8,128)} %shard_map.55) | data formatting | bytes 65536

commit v6 on v5

--- a/solution.py
+++ b/solution.py
@@ -166,6 +166,11 @@
     def product(c, labels):
         wide = quick(w_high[c], labels)
         return wide[:, :half] + wide[:, half:] + quick(w_low[c], labels[:, :half])
+
+    def whole_product(labels):
+        wide = quick(w_high[...].reshape(cols * pair, n_cols), labels)
+        low = quick(w_low[...].reshape(cols * pair, n_cols), labels[:, :half])
+        return (wide[:, :half] + wide[:, half:] + low).reshape(cols, pair, half)
 
     def block(c):
         ours = row_emb[c]
@@ -217,10 +222,9 @@
         if step < ITERS - 1:
             depth = pair + AUX if step == 0 else pair
             if step > 0:
+                part[step, :, :pair] = whole_product(labels)
                 for other in reversed(others_z):
-                    part[step, other, :pair] = product(other, labels)
                     send_part(step, other, depth)
-                part[step, z, :pair] = product(z, labels)
             total = part[step, z, :depth]
             for other in others_z:
                 arrived(summed.at[step, other, pl.ds(0, depth)], sum_sem.at[step, other])
@@ -236,11 +240,10 @@
             for other in others_chip:
                 arrived(later.at[step, other], later_sem.at[step, other])
         else:
+            last_part[...] = whole_product(labels).reshape(cols, 2, piece, half)
             for other in reversed(others_z):
-                last_part[other] = product(other, labels).reshape(2, piece, half)
                 for k in range(2):
                     push(last_part.at[other, k], last.at[z, core], last_sem.at[z, core], (2 * chip + k, other))
-            last_part[z] = product(z, labels).reshape(2, piece, half)
             push(last_part.at[z, 1 - core], last.at[z, core], last_sem.at[z, core], (twin, z))
             last[z, core] = last_part[z, core]
             arrived(last.at[z, 1 - core], last_sem.at[z, 1 - core])

time: 42.3 us -> 42.4 us (level)
  no operation moved by 1% of the time
where the time goes in v6:
time: 42.4 us; the launch traced here: 42.2 us
  Pallas kernels  40.8 us (96%)
  local copies, waits for them, and re-layouts  1.38 us (3%)
    pallas_call x1, Pallas kernels, local(): pl.pallas_call(functools.partial(kernel, chips, cols), out_shape=jax.Shap...  40.8 us
    unnamed x1, local copies, waits for them, and re-layouts  1.38 us

profile of v6, /device:TPU:0, one launch (start us, length us, event | category | flops | bytes accessed | tf_op | source)
XLA Modules:
  0.0 42.2 jit_solution(1806328092360848103)
XLA Ops:
  0.0 40.8 %shard_map.55 = f32[32,256]{1,0:T(8,128)} custom-call(f32[32,768]{1,0:T(8,128)} %emb_ref.1, f32[1,32]{1,0:T(1,128)} %bitcast.2, f32[32,256]{1,0:T(8,128)} %soft_ref.1, s32[1,32]{1,0:T(1,128)} %bitcast.3, s32[4,32]{1,0:T(4,128)} %tile_ref.1), custom_call_target="tpu_custom_call" | custom-call | tf_op jit(solution)/shard_map/pallas_call | solution.py:277
  40.8 1.4 %copy.7 = f32[32,256]{1,0:T(8,128)} copy(f32[32,256]{1,0:T(8,128)} %shard_map.55) | data formatting | bytes 65536
